TPU v7x, 32 devices: a whole 2x2x4 slice. The times are simulated.
32 devices in a mesh: dp: 2 (over core), expert: 16 (over z, y, x).
Axes of the slice: x: 2, y: 2, z: 4, core: 2. Of those that a mesh axis runs over, the one named last changes fastest.
Arguments:
- tokens: bfloat16 [2048, 4096], P('expert', 'dp'), may hold values from -6 to 6
- gates: float32 [2048, 8], P('expert'), may hold values from 0.03 to 0.5
- expert_ids: int32 [2048, 8], P('expert'), may hold values from 0 to 15, as said below
- d_mixed: bfloat16 [2048, 4096], P('expert', 'dp'), may hold values from -6 to 6
- w_up: bfloat16 [16, 4096, 1024], P('expert', 'dp'), may hold values from -0.09375 to 0.09375
- w_down: bfloat16 [16, 1024, 4096], P('expert', None, 'dp'), may hold values from -0.1875 to 0.1875
Outputs:
- mixed: bfloat16 [2048, 4096], P('expert', 'dp')
- d_tokens: bfloat16 [2048, 4096], P('expert', 'dp')
- grad_up: bfloat16 [16, 4096, 1024], P('expert', 'dp')
- grad_down: bfloat16 [16, 1024, 4096], P('expert', None, 'dp')
Inputs may be any that keep to these rules, and one draw needn't show every extreme that they name: `expert_ids`: each row names 8 different experts. In the tokens of one device (aligned blocks of 128 rows) one expert, the same for every device, is named by exactly 64 tokens, and every other expert by at most 64 tokens; both bounds are reached on every device.
All inputs are finite; a program needn't handle non-finite values.
Results may differ from a plain program's by a relative error of at most 0.025.
Values may be sent and summed in bfloat16 or wider, within the bound.
A program may use at most 128 MiB of HBM per device.

v0:
```python
import jax
import jax.numpy as jnp
from jax import lax
from jax.sharding import PartitionSpec as P


def row_product(row_block, first_weight):
    first_rows = jnp.dot(row_block, first_weight, preferred_element_type=jnp.float32)
    return first_rows


def transposed_product(row_block, first_weight):
    contract = (((1,), (1,)), ((), ()))
    first_rows = lax.dot_general(
        row_block, first_weight, contract, preferred_element_type=jnp.float32
    )
    return first_rows


def outer_sum(left_rows, right_rows):
    return lax.dot_general(
        left_rows, right_rows, (((0,), (0,)), ((), ())), preferred_element_type=jnp.float32
    )


def per_device(tokens, gates, expert_ids, d_mixed, w_up, w_down):
    tok_rows, features = tokens.shape
    top_count = expert_ids.shape[1]
    groups = lax.axis_size("expert")
    pair_count = tok_rows * top_count
    hot_rows = tok_rows // 2
    cold_rows = (pair_count - hot_rows + groups - 2) // (groups - 1)
    routed = expert_ids.reshape(pair_count)
    onehot = (routed[:, None] == jnp.arange(groups, dtype=jnp.int32)[None, :]).astype(jnp.int32)
    order_in = jnp.sum((jnp.cumsum(onehot, 0) - onehot) * onehot, 1)
    up_home = w_up[0]
    down_home = w_down[0]
    capacity = max(hot_rows, cold_rows)
    local_rows = 0
    slot_index = routed * capacity + order_in
    sent_rows = groups * capacity
    all_rows = sent_rows + local_rows
    source = (
        jnp.full((all_rows,), pair_count, jnp.int32)
        .at[slot_index]
        .set(jnp.arange(pair_count, dtype=jnp.int32))
    )
    token_index = jnp.where(source < pair_count, source // top_count, tok_rows)
    zero_row = jnp.zeros((1, features), jnp.bfloat16)
    scaled = (
        (gates[:, :, None] * d_mixed[:, None, :].astype(jnp.float32))
        .astype(jnp.bfloat16)
        .reshape(pair_count, features)
    )
    rows_in = jnp.concatenate([tokens, zero_row], 0)[token_index]
    scaled_in = jnp.concatenate([scaled, zero_row], 0)[source]
    remote_rows, remote_scaled = (
        lax.all_to_all(
            rows_in.reshape(groups, capacity, features),
            "expert",
            split_axis=0,
            concat_axis=0,
            tiled=True,
        ),
        lax.all_to_all(
            scaled_in.reshape(groups, capacity, features),
            "expert",
            split_axis=0,
            concat_axis=0,
            tiled=True,
        ),
    )
    rows_all = jnp.concatenate([remote_rows.reshape(sent_rows, features), rows_in[sent_rows:]], 0)
    scaled_all = jnp.concatenate(
        [remote_scaled.reshape(sent_rows, features), scaled_in[sent_rows:]], 0
    )
    up_part = row_product(rows_all, up_home).astype(jnp.bfloat16)
    back_part = transposed_product(scaled_all, down_home).astype(jnp.bfloat16)
    pre_share, back_share = (
        lax.psum_scatter(up_part, "dp", scatter_dimension=0, tiled=True).astype(jnp.float32),
        lax.psum_scatter(back_part, "dp", scatter_dimension=0, tiled=True).astype(jnp.float32),
    )
    logistic = jax.nn.sigmoid(pre_share)
    hidden_share = jax.nn.silu(pre_share).astype(jnp.bfloat16)
    grad_share = (back_share * logistic * (1.0 + pre_share * (1.0 - logistic))).astype(jnp.bfloat16)
    hidden, grad_pre = (
        lax.all_gather(hidden_share, "dp", axis=0, tiled=True),
        lax.all_gather(grad_share, "dp", axis=0, tiled=True),
    )
    expert_out = row_product(hidden, down_home).astype(jnp.bfloat16)
    grad_in = transposed_product(grad_pre, up_home).astype(jnp.bfloat16)
    back_out, back_in = (
        lax.all_to_all(
            expert_out.reshape(groups, capacity, features),
            "expert",
            split_axis=0,
            concat_axis=0,
            tiled=True,
        ),
        lax.all_to_all(
            grad_in.reshape(groups, capacity, features),
            "expert",
            split_axis=0,
            concat_axis=0,
            tiled=True,
        ),
    )
    out_table = jnp.concatenate([back_out.reshape(sent_rows, features), expert_out[sent_rows:]], 0)
    in_table = jnp.concatenate([back_in.reshape(sent_rows, features), grad_in[sent_rows:]], 0)
    pair_out = out_table[slot_index].reshape(tok_rows, top_count, features).astype(jnp.float32)
    mixed_out = jnp.sum(gates[:, :, None] * pair_out, 1).astype(jnp.bfloat16)
    pair_in = in_table[slot_index].reshape(tok_rows, top_count, features).astype(jnp.float32)
    tokens_grad = jnp.sum(pair_in, 1).astype(jnp.bfloat16)
    up_total = outer_sum(rows_all, grad_pre)
    down_total = outer_sum(hidden, scaled_all)
    return (
        mixed_out,
        tokens_grad,
        up_total.astype(jnp.bfloat16)[None],
        down_total.astype(jnp.bfloat16)[None],
    )


def solution(mesh):
    in_specs = (
        P("expert", "dp"),
        P("expert", None),
        P("expert", None),
        P("expert", "dp"),
        P("expert", "dp", None),
        P("expert", None, "dp"),
    )
    out_specs = (
        P("expert", "dp"),
        P("expert", "dp"),
        P("expert", "dp", None),
        P("expert", None, "dp"),
    )
    return jax.shard_map(
        per_device, mesh=mesh, in_specs=in_specs, out_specs=out_specs, check_vma=False
    )
```

profile of v0, /device:TPU:12, one launch (start us, length us, event | category | flops | bytes accessed | tf_op | source)
XLA Modules:
  0.0 503.1 jit_solution(12961521910105347370)
XLA Ops:
  7.2 0.7 broadcast_multiply_fusion
  7.9 0.8 copy.15
  9.0 0.8 copy.13
  9.9 4.5 reduce-window.6
  14.9 4.3 scatter_custom_fusion
  19.3 1.1 convert_element_type.65
  20.4 0.9 fusion.1
  21.3 2.3 concatenate.7
  23.6 11.6 %gather_fusion.2 = bf16[1024,2048]{1,0:T(8,128)(2,1)} fusion(bf16[1025,2048]{1,0:T(8,128)(2,1)} %concatenate.7, s32[1024]{0:T(1024)S(1)} %get-tuple-element.6), kind=kCustom, calls=%fused_computation.2 | custom fusion | bytes 8392704 | tf_op jit(solution)/shard_map/gather | solution.py:56
  35.1 7.3 %all-to-all-start.2 = ((bf16[16,64,2048]{2,1,0:T(8,128)(2,1)}), bf16[16,64,2048]{2,1,0:T(8,128)(2,1)}, u32[]{:S(2)}, u32[]{:S(2)}) async-start(bf16[16,64,2048]{2,1,0:T(8,128)(2,1)} %bitcast.69), calls=%async_computation.3 | async-start | bytes 8388608 | tf_op jit(solution)/shard_map/all_to_all | solution.py:65
  42.5 6.0 %gather_fusion = bf16[1024,2048]{1,0:T(8,128)(2,1)} fusion(bf16[129,2048]{1,0:T(8,128)(2,1)S(1)} %concatenate.6, s32[1024]{0:T(1024)S(1)} %get-tuple-element.7), kind=kCustom, calls=%fused_computation | custom fusion | bytes 8392704 | tf_op jit(solution)/shard_map/gather | solution.py:55
  48.5 88.2 %all-to-all-done.2 = bf16[16,64,2048]{2,1,0:T(8,128)(2,1)} async-done(((bf16[16,64,2048]{2,1,0:T(8,128)(2,1)}), bf16[16,64,2048]{2,1,0:T(8,128)(2,1)}, u32[]{:S(2)}, u32[]{:S(2)}) %all-to-all-start.2) | async-done | bytes 4194336 | tf_op jit(solution)/shard_map/all_to_all | solution.py:65
  136.7 5.6 %all-to-all-start = ((bf16[16,64,2048]{2,1,0:T(8,128)(2,1)}), bf16[16,64,2048]{2,1,0:T(8,128)(2,1)}, u32[]{:S(2)}, u32[]{:S(2)}) async-start(bf16[16,64,2048]{2,1,0:T(8,128)(2,1)} %bitcast.68), calls=%async_computation | async-start | bytes 8388608 | tf_op jit(solution)/shard_map/all_to_all | solution.py:58
  142.3 9.3 %fusion.26 = bf16[1024,1024]{1,0:T(8,128)(2,1)} fusion(bf16[1024,2048]{1,0:T(8,128)(2,1)} %bitcast.13, bf16[1,1024,2048]{2,1,0:T(8,128)(2,1)} %param.11), kind=kOutput, calls=%fused_computation.33 | convolution fusion | flops 4296015872 | bytes 10485760 | tf_op jit(solution)/shard_map/dot_general | solution.py:14
  151.7 82.7 %all-to-all-done = bf16[16,64,2048]{2,1,0:T(8,128)(2,1)} async-done(((bf16[16,64,2048]{2,1,0:T(8,128)(2,1)}), bf16[16,64,2048]{2,1,0:T(8,128)(2,1)}, u32[]{:S(2)}, u32[]{:S(2)}) %all-to-all-start) | async-done | bytes 4194336 | tf_op jit(solution)/shard_map/all_to_all | solution.py:58
  234.3 9.3 %fusion.23 = bf16[1024,1024]{1,0:T(8,128)(2,1)} fusion(bf16[1024,2048]{1,0:T(8,128)(2,1)} %bitcast.5, bf16[1,2048,1024]{2,1,0:T(8,128)(2,1)} %param.10), kind=kOutput, calls=%fused_computation.32 | convolution fusion | flops 4296015872 | bytes 10485760 | tf_op jit(solution)/shard_map/dot_general | solution.py:8
  243.9 9.4 %reduce-scatter.3.cloned.1.call-done = bf16[512,1024]{1,0:T(8,128)(2,1)} async-done(((bf16[1024,1024]{1,0:T(8,128)(2,1)}), bf16[512,1024]{1,0:T(8,128)(2,1)}) %reduce-scatter.3.cloned.1.call-update) | async-done | bytes 1048592 | tf_op jit(solution)/shard_map/reduce_scatter | solution.py:80
  253.3 4.0 fusion.22
  257.3 11.9 %all-gather.3.cloned.1.call-done = bf16[1024,1024]{1,0:T(8,128)(2,1)} async-done(((bf16[512,1024]{1,0:T(8,128)(2,1)}), bf16[1024,1024]{1,0:T(8,128)(2,1)}) %all-gather.3.cloned.1.call-update) | async-done | bytes 2097168 | tf_op jit(solution)/shard_map/all_gather | solution.py:87
  269.2 9.3 %fusion.13 = bf16[1024,2048]{1,0:T(8,128)(2,1)} fusion(bf16[1024,1024]{1,0:T(8,128)(2,1)} %all-gather.3.cloned.1.call-done, bf16[1,1024,2048]{2,1,0:T(8,128)(2,1)} %param.11), kind=kOutput, calls=%fused_computation.21 | convolution fusion | flops 4297064448 | bytes 10485760 | tf_op jit(solution)/shard_map/dot_general | solution.py:8
  278.5 7.0 %all-to-all-start.1 = ((bf16[16,64,2048]{2,1,0:T(8,128)(2,1)}), bf16[16,64,2048]{2,1,0:T(8,128)(2,1)}, u32[]{:S(2)}, u32[]{:S(2)}) async-start(bf16[16,64,2048]{2,1,0:T(8,128)(2,1)} %bitcast.71), calls=%async_computation.2 | async-start | bytes 8388608 | tf_op jit(solution)/shard_map/all_to_all | solution.py:93
  286.0 13.8 %all-gather.5.cloned.1.call-done = bf16[1024,1024]{1,0:T(8,128)(2,1)} async-done(((bf16[512,1024]{1,0:T(8,128)(2,1)}), bf16[1024,1024]{1,0:T(8,128)(2,1)}) %all-gather.5.cloned.1.call-update) | async-done | bytes 2097168 | tf_op jit(solution)/shard_map/all_gather | solution.py:88
  299.8 9.3 %fusion.10 = bf16[1024,2048]{1,0:T(8,128)(2,1)} fusion(bf16[1024,1024]{1,0:T(8,128)(2,1)} %all-gather.5.cloned.1.call-done, bf16[1,2048,1024]{2,1,0:T(8,128)(2,1)} %param.10), kind=kOutput, calls=%fused_computation.20 | convolution fusion | flops 4297064448 | bytes 10485760 | tf_op jit(solution)/shard_map/dot_general | solution.py:14
  309.1 71.4 %all-to-all-done.1 = bf16[16,64,2048]{2,1,0:T(8,128)(2,1)} async-done(((bf16[16,64,2048]{2,1,0:T(8,128)(2,1)}), bf16[16,64,2048]{2,1,0:T(8,128)(2,1)}, u32[]{:S(2)}, u32[]{:S(2)}) %all-to-all-start.1) | async-done | bytes 4194336 | tf_op jit(solution)/shard_map/all_to_all | solution.py:93
  380.6 6.1 %all-to-all-start.3 = ((bf16[16,64,2048]{2,1,0:T(8,128)(2,1)}), bf16[16,64,2048]{2,1,0:T(8,128)(2,1)}, u32[]{:S(2)}, u32[]{:S(2)}) async-start(bf16[16,64,2048]{2,1,0:T(8,128)(2,1)} %bitcast.70), calls=%async_computation.5 | async-start | bytes 8388608 | tf_op jit(solution)/shard_map/all_to_all | solution.py:100
  386.7 8.5 %convert_bitcast_fusion.1 = bf16[1,2048,1024]{2,1,0:T(8,128)(2,1)} fusion(bf16[1024,2048]{1,0:T(8,128)(2,1)} %bitcast.5, bf16[1024,1024]{1,0:T(8,128)(2,1)S(1)} %copy-done.2), kind=kOutput, calls=%fused_computation.19 | convolution fusion | flops 4297064448 | bytes 10485760 | tf_op jit(solution)/shard_map/dot_general | solution.py:21
  395.2 8.3 %convert_bitcast_fusion = bf16[1,1024,2048]{2,1,0:T(8,128)(2,1)} fusion(bf16[1024,1024]{1,0:T(8,128)(2,1)S(1)} %copy-done.1, bf16[1024,2048]{1,0:T(8,128)(2,1)} %bitcast.13), kind=kOutput, calls=%fused_computation.18 | convolution fusion | flops 4297064448 | bytes 10485760 | tf_op jit(solution)/shard_map/dot_general | solution.py:21
  403.6 11.5 %gather_fusion.1 = bf16[1024,2048]{1,0:T(8,128)(2,1)} fusion(bf16[1024,2048]{1,0:T(8,128)(2,1)} %bitcast.9, s32[1024]{0:T(1024)S(1)} %broadcast_clamp_fusion), kind=kCustom, calls=%fused_computation.1 | custom fusion | bytes 8392704 | tf_op jit(solution)/shard_map/gather | solution.py:110
  415.1 7.3 %fusion = bf16[128,2048]{1,0:T(8,128)(2,1)} fusion(bf16[1024,2048]{1,0:T(8,128)(2,1)} %gather_fusion.1, f32[128,8]{1,0:T(8,128)S(1)} %copy.13), kind=kLoop, calls=%fused_computation.6 | loop fusion | flops 6029312 | bytes 4722688 | tf_op jit(solution)/shard_map/reduce_sum | solution.py:111
  422.4 56.7 %all-to-all-done.3 = bf16[16,64,2048]{2,1,0:T(8,128)(2,1)} async-done(((bf16[16,64,2048]{2,1,0:T(8,128)(2,1)}), bf16[16,64,2048]{2,1,0:T(8,128)(2,1)}, u32[]{:S(2)}, u32[]{:S(2)}) %all-to-all-start.3) | async-done | bytes 4194336 | tf_op jit(solution)/shard_map/all_to_all | solution.py:100
  479.2 11.5 %gather_fusion.3 = bf16[1024,2048]{1,0:T(8,128)(2,1)} fusion(bf16[1024,2048]{1,0:T(8,128)(2,1)} %bitcast.15, s32[1024]{0:T(1024)S(1)} %broadcast_clamp_fusion), kind=kCustom, calls=%fused_computation.3 | custom fusion | bytes 8392704 | tf_op jit(solution)/shard_map/gather | solution.py:112
  490.7 5.9 %bitcast_reduce_fusion = bf16[128,2048]{1,0:T(8,128)(2,1)} fusion(bf16[1024,2048]{1,0:T(8,128)(2,1)} %gather_fusion.3), kind=kLoop, calls=%fused_computation.9 | loop fusion | flops 1835008 | bytes 4718592 | tf_op jit(solution)/shard_map/reduce_sum | solution.py:113
  (33 shorter events, 1.9 us)
Async XLA Ops:
  35.1 7.3 %copy-start = (bf16[128,2048]{1,0:T(8,128)(2,1)S(1)}, bf16[128,2048]{1,0:T(8,128)(2,1)}, u32[]{:S(2)}) copy-start(bf16[128,2048]{1,0:T(8,128)(2,1)} %param.6) | copy-start | bytes 1572868
  35.1 101.5 %all-to-all-start.2 = ((bf16[16,64,2048]{2,1,0:T(8,128)(2,1)}), bf16[16,64,2048]{2,1,0:T(8,128)(2,1)}, u32[]{:S(2)}, u32[]{:S(2)}) async-start(bf16[16,64,2048]{2,1,0:T(8,128)(2,1)} %bitcast.69), calls=%async_computation.3 | async-start | bytes 8388608 | tf_op jit(solution)/shard_map/all_to_all | solution.py:65
  136.7 97.7 %all-to-all-start = ((bf16[16,64,2048]{2,1,0:T(8,128)(2,1)}), bf16[16,64,2048]{2,1,0:T(8,128)(2,1)}, u32[]{:S(2)}, u32[]{:S(2)}) async-start(bf16[16,64,2048]{2,1,0:T(8,128)(2,1)} %bitcast.68), calls=%async_computation | async-start | bytes 8388608 | tf_op jit(solution)/shard_map/all_to_all | solution.py:58
  142.2 101.7 %reduce-scatter.5.cloned.1.call-start = ((), (), s32[]{:S(2)}) async-start(), calls=%async_computation.8 | async-start | bytes 3145728 | tf_op jit(solution)/shard_map/reduce_scatter | solution.py:81
  151.6 101.7 %reduce-scatter.3.cloned.1.call-start = ((), (), s32[]{:S(2)}) async-start(), calls=%async_computation.6 | async-start | bytes 3145728 | tf_op jit(solution)/shard_map/reduce_scatter | solution.py:80
  243.6 25.5 %all-gather.3.cloned.1.call-start = ((), (), s32[]{:S(2)}) async-start(), calls=%async_computation.7 | async-start | bytes 3145728 | tf_op jit(solution)/shard_map/all_gather | solution.py:87
  278.5 102.1 %all-to-all-start.1 = ((bf16[16,64,2048]{2,1,0:T(8,128)(2,1)}), bf16[16,64,2048]{2,1,0:T(8,128)(2,1)}, u32[]{:S(2)}, u32[]{:S(2)}) async-start(bf16[16,64,2048]{2,1,0:T(8,128)(2,1)} %bitcast.71), calls=%async_computation.2 | async-start | bytes 8388608 | tf_op jit(solution)/shard_map/all_to_all | solution.py:93
  285.5 14.4 %all-gather.5.cloned.1.call-start = ((), (), s32[]{:S(2)}) async-start(), calls=%async_computation.9 | async-start | bytes 3145728 | tf_op jit(solution)/shard_map/all_gather | solution.py:88
  380.6 6.2 %copy-start.2 = (bf16[1024,1024]{1,0:T(8,128)(2,1)S(1)}, bf16[1024,1024]{1,0:T(8,128)(2,1)}, u32[]{:S(2)}) copy-start(bf16[1024,1024]{1,0:T(8,128)(2,1)} %all-gather.5.cloned.1.call-done) | copy-start | bytes 6291460
  380.6 98.6 %all-to-all-start.3 = ((bf16[16,64,2048]{2,1,0:T(8,128)(2,1)}), bf16[16,64,2048]{2,1,0:T(8,128)(2,1)}, u32[]{:S(2)}, u32[]{:S(2)}) async-start(bf16[16,64,2048]{2,1,0:T(8,128)(2,1)} %bitcast.70), calls=%async_computation.5 | async-start | bytes 8388608 | tf_op jit(solution)/shard_map/all_to_all | solution.py:100
  386.7 8.5 %copy-start.1 = (bf16[1024,1024]{1,0:T(8,128)(2,1)S(1)}, bf16[1024,1024]{1,0:T(8,128)(2,1)}, u32[]{:S(2)}) copy-start(bf16[1024,1024]{1,0:T(8,128)(2,1)} %all-gather.3.cloned.1.call-done) | copy-start | bytes 6291460
Sparse Core Ops, SparseCore 0:
  151.7 10.7 reduce-scatter.4
  243.8 9.4 reduce-scatter.2
  257.4 11.7 all-gather.2
  288.1 11.6 all-gather.4
where the time goes:
time: 504 us; the launch traced here: 503 us
  waiting for transfers between devices  335 us (66%)
  matrix products  54 us (11%)
  local copies, waits for them, and re-layouts  49.6 us (10%)
  starting transfers between devices  26.3 us (5%)
  other arithmetic  24.6 us (5%)
  between operations  13.9 us (3%)
    all_to_all x1, waiting for transfers between devices, per_device(): lax.all_to_all(scaled_in.reshape(groups, capacity, features), 'expert', s...  88.2 us
    all_to_all x1, waiting for transfers between devices, per_device(): lax.all_to_all(rows_in.reshape(groups, capacity, features), 'expert', spl...  82.7 us
    all_to_all x1, waiting for transfers between devices, per_device(): lax.all_to_all(expert_out.reshape(groups, capacity, features), 'expert',...  71.4 us
    all_to_all x1, waiting for transfers between devices, per_device(): lax.all_to_all(grad_in.reshape(groups, capacity, features), 'expert', spl...  56.7 us
    dot_general x2, matrix products, transposed_product(): lax.dot_general(row_block, first_weight, contract, preferred_element_type...  18.6 us
    dot_general x2, matrix products, row_product(): jnp.dot(row_block, first_weight, preferred_element_type=jnp.float32)  18.6 us
    dot_general x2, matrix products, outer_sum(): lax.dot_general(left_rows, right_rows, (((0,), (0,)), ((), ())), preferre...  16.8 us
    all_gather x1, waiting for transfers between devices, per_device(): lax.all_gather(grad_share, 'dp', axis=0, tiled=True)  13.8 us
  transfers between devices with their start and end apart: 8, of which 7 were waited for; matrix products, arithmetic and copies ran while one was open for 14% of the time, Pallas kernels for 0%

commit v1 on v0

v1 whole, which is shorter than its diff:
```python
import functools

import jax
import jax.numpy as jnp
from jax import lax
from jax.experimental import pallas as pl
from jax.experimental.pallas import tpu as pltpu
from jax.sharding import PartitionSpec as P

MESH = pl.DeviceIdType.MESH
F32 = jnp.float32
BF16 = jnp.bfloat16


def tiles(extent, size, body):
    size = min(size, extent)

    def step(j, carry):
        body(pl.multiple_of(j * size, size), size)
        return carry

    lax.fori_loop(0, extent // size, step, 0)


def flip(value, mask, limit):
    result = value
    bit = 1
    while bit < limit:
        on = (mask // bit) % 2
        result = result + bit * on * (1 - 2 * ((value // bit) % 2))
        bit *= 2
    return result


def mm(a, b, da, db):
    return lax.dot_general(a, b, (((da,), (db,)), ((), ())), preferred_element_type=F32)


def kernel(
    cfg,
    tok, gates, ids, dmix, w_up, w_down,
    mixed, dtok, grad_up, grad_down,
    gt, sx, rows, wu, wd, part, rsbuf, hid, pre, own, cx, cy, cz, mt, mx,
    zs, zr, mzs, mzr, ys, yr, mys, myr, xs, xr, mxs, mxr,
    rss, rsr, ags, agr, cxs, cxr, cys, cyr, czs, czr, loc,
):
    groups, nd, t_rows, top, feat, ff, cap = cfg
    planes = groups // 4
    count = 2 * planes
    half = 2 * cap
    chunk = 4 * cap
    share = chunk // nd
    e = lax.axis_index("expert")
    me = lax.axis_index("dp")
    z, y, x = e // 4, (e // 2) % 2, e % 2
    e_x = e + 1 - 2 * x
    e_y = e + 2 - 4 * y

    def ring_of(i):
        return (i + i // planes) % planes

    def z_peer(r):
        return flip(z, r, planes) * 4 + y * 2 + x

    def send(src, dst, ssem, rsem, expert=None, dp=None):
        where = {"expert": expert} if dp is None else {"dp": dp}
        return pltpu.make_async_remote_copy(
            src_ref=src, dst_ref=dst, send_sem=ssem, recv_sem=rsem,
            device_id=where, device_id_type=MESH,
        )

    def z_copy(i, src):
        return send(src, gt.at[i, 0], zs.at[i], zr.at[i], z_peer(ring_of(i)))

    def mz_copy(i):
        return send(mt.at[0, 0], mt.at[i, 0], mzs.at[i], mzr.at[i], z_peer(ring_of(i)))

    def y_copy(i):
        return send(gt.at[i, 0], gt.at[i, 1], ys.at[i], yr.at[i], e_y)

    def my_copy(i):
        return send(mt.at[i, 0], mt.at[i, 1], mys.at[i], myr.at[i], e_y)

    def x_copy(i, yy):
        return send(
            sx.at[i, pl.ds(yy * cap, cap)], rows.at[i, pl.ds(half + yy * cap, cap)],
            xs.at[i, yy], xr.at[i, yy], e_x,
        )

    def mx_copy(i, yy):
        return send(mt.at[i, yy], mx.at[i, yy], mxs.at[i, yy], mxr.at[i, yy], e_x)

    def rs_copy(i, o):
        peer = (me + o) % nd
        return send(
            part.at[i % 2, pl.ds(pl.multiple_of(peer * share, share), share)],
            rsbuf.at[i, o - 1], rss.at[i, o - 1], rsr.at[i, o - 1], dp=peer,
        )

    def ag_copy(i, o):
        mine = hid.at[i, pl.ds(pl.multiple_of(me * share, share), share)]
        return send(mine, mine, ags.at[i, o - 1], agr.at[i, o - 1], dp=(me + o) % nd)

    def cx_copy(i):
        return send(sx.at[i], cx.at[i], cxs.at[i], cxr.at[i], e_x)

    def cy_copy(i):
        return send(gt.at[i, 1], cy.at[i], cys.at[i], cyr.at[i], e_y)

    def cz_copy(i):
        return send(gt.at[i, 0], cz.at[i], czs.at[i], czr.at[i], z_peer(ring_of(i)))

    tok_in = pltpu.make_async_copy(tok, gt.at[0, 0], loc.at[0])
    dmix_in = pltpu.make_async_copy(dmix, gt.at[count - 1, 0], loc.at[1])
    wu_in = pltpu.make_async_copy(w_up.at[0], wu, loc.at[2])
    wd_in = pltpu.make_async_copy(w_down.at[0], wd, loc.at[3])
    tok_in.start()
    dmix_in.start()
    wu_in.start()
    wd_in.start()

    barrier = pltpu.get_barrier_semaphore()
    peers = [{"expert": z_peer(r)} for r in range(1, planes)]
    peers += [{"expert": e_x}, {"expert": e_y}]
    peers += [{"dp": (me + o) % nd} for o in range(1, nd)]
    for peer in peers:
        pl.semaphore_signal(barrier, inc=1, device_id=peer, device_id_type=MESH)
    pl.semaphore_wait(barrier, len(peers))

    for i in range(1, planes):
        z_copy(i, tok).start()

    lane = lax.broadcasted_iota(jnp.int32, (t_rows, t_rows), 1)
    row = lax.broadcasted_iota(jnp.int32, (t_rows, t_rows), 0)
    chosen = jnp.zeros((t_rows, t_rows), F32)
    weight = jnp.zeros((t_rows, t_rows), F32)
    for k in range(top):
        hit = ids[:, k : k + 1] == lane
        chosen = chosen + jnp.where(hit, 1.0, 0.0)
        weight = weight + jnp.where(hit, gates[:, k : k + 1], 0.0)
    before = jnp.where(lane < row, 1.0, 0.0).astype(BF16)
    place = mm(before, chosen.astype(BF16), 1, 0)
    place = jnp.where(chosen > 0.0, place, -1.0)
    mt[0, 0, :groups, :] = jnp.transpose(place)[:groups]
    mt[0, 0, groups:, :] = jnp.transpose(weight)[:groups]
    for i in range(1, planes):
        mz_copy(i).start()

    slot = lax.broadcasted_iota(jnp.int32, (cap, t_rows), 0).astype(F32)

    def pick(table, expert):
        hot = slot == table[pl.ds(expert, 1), :]
        gate = jnp.sum(jnp.where(hot, table[pl.ds(groups + expert, 1), :], 0.0), 1, keepdims=True)
        return jnp.where(hot, 1.0, 0.0).astype(BF16), gate

    def select(i, yy):
        r = ring_of(i)
        hot_n, gate_n = pick(mt.at[r, yy], e_x)
        hot_o, gate_o = pick(mt.at[r, yy], e)
        hot = jnp.concatenate([hot_n, hot_o], 0)
        gate = jnp.concatenate([gate_n, gate_o], 0)
        gate = jnp.where(i < planes, 1.0, gate)

        def tile(at, size):
            got = mm(hot, gt[i, yy, :, pl.ds(at, size)], 1, 0) * gate
            got = got.astype(BF16)
            sx[i, yy * cap : (yy + 1) * cap, pl.ds(at, size)] = got[:cap]
            rows[i, yy * cap : (yy + 1) * cap, pl.ds(at, size)] = got[cap:]

        tiles(feat, 512, tile)
        x_copy(i, yy).start()

        @pl.when(i < planes)
        def _():
            mx_copy(i, yy).start()

    def stage_z(i):
        @pl.when(i == 0)
        def _():
            tok_in.wait()

        @pl.when(i == count - 1)
        def _():
            dmix_in.wait()

        @pl.when(ring_of(i) != 0)
        def _():
            z_copy(i, tok).wait_recv()

            @pl.when(i < planes)
            def _():
                mz_copy(i).wait_recv()

        y_copy(i).start()

        @pl.when(i < planes)
        def _():
            my_copy(i).start()

        @pl.when(i < planes - 1)
        def _():
            z_copy(i + planes, dmix).start()

    def stage_y(i):
        y_copy(i).wait()

        @pl.when(i < planes)
        def _():
            my_copy(i).wait()

        select(i, 1)

    def stage_in(i):
        for yy in range(2):
            x_copy(i, yy).wait()

        @pl.when(i < planes)
        def _():
            for yy in range(2):
                mx_copy(i, yy).wait()

            @pl.when(i == 0)
            def _():
                wu_in.wait()

            def tile(at, size):
                part[i % 2, :, pl.ds(at, size)] = mm(
                    rows[i], wu[:, pl.ds(at, size)], 1, 0
                ).astype(BF16)

            tiles(ff, 256, tile)

        @pl.when(i >= planes)
        def _():
            def tile(at, size):
                part[i % 2, :, pl.ds(at, size)] = mm(
                    rows[i], wd[pl.ds(at, size), :], 1, 1
                ).astype(BF16)

            tiles(ff, 256, tile)

        for o in range(1, nd):
            rs_copy(i, o).start()

    def stage_act(i):
        for o in range(1, nd):
            rs_copy(i, o).wait()
        r = ring_of(i)
        base = me * share

        def tile(at, size):
            here = pl.ds(pl.multiple_of(base + at, size), size)
            total = part[i % 2, here, :].astype(F32)
            for o in range(1, nd):
                total = total + rsbuf[i, o - 1, pl.ds(at, size), :].astype(F32)

            @pl.when(i < planes)
            def _():
                pre[r, pl.ds(at, size), :] = total
                hid[i, here, :] = (total / (1.0 + jnp.exp(-total))).astype(BF16)

            @pl.when(i >= planes)
            def _():
                value = pre[r, pl.ds(at, size), :]
                s = 1.0 / (1.0 + jnp.exp(-value))
                hid[i, here, :] = (total * s * (1.0 + value * (1.0 - s))).astype(BF16)

        tiles(share, 16, tile)
        for o in range(1, nd):
            ag_copy(i, o).start()

    def stage_out(i):
        for o in range(1, nd):
            ag_copy(i, o).wait()

        def store(at, size, got):
            got = got.astype(BF16)
            own[i % 2, :, pl.ds(at, size)] = got[:half]
            sx[i, :, pl.ds(at, size)] = got[half:]

        @pl.when(i < planes)
        def _():
            @pl.when(i == 0)
            def _():
                wd_in.wait()

            gate = jnp.concatenate(
                [pick(t.at[i, yy], e)[1] for t in (mt, mx) for yy in range(2)], 0
            )

            def tile(at, size):
                store(at, size, mm(hid[i], wd[:, pl.ds(at, size)], 1, 0) * gate)

            tiles(feat, 256, tile)

        @pl.when(i >= planes)
        def _():
            def tile(at, size):
                store(at, size, mm(hid[i], wu[pl.ds(at, size), :], 1, 1))

            tiles(feat, 256, tile)

        cx_copy(i).start()

    def stage_cx(i):
        cx_copy(i).wait()
        r = ring_of(i)
        for yy in (1, 0):
            hot = jnp.concatenate([pick(mt.at[r, yy], e)[0], pick(mt.at[r, yy], e_x)[0]], 0)

            def tile(at, size):
                there = slice(yy * cap, (yy + 1) * cap)
                data = jnp.concatenate(
                    [own[i % 2, there, pl.ds(at, size)], cx[i, there, pl.ds(at, size)]], 0
                )
                gt[i, yy, :, pl.ds(at, size)] = mm(hot, data, 0, 0).astype(BF16)

            tiles(feat, 512, tile)
            if yy == 1:
                cy_copy(i).start()

    def stage_cy(i):
        cy_copy(i).wait()

        def tile(at, size):
            here = pl.ds(at, size)
            total = gt[i, 0, here, :].astype(F32) + cy[i, here, :].astype(F32)
            gt[i, 0, here, :] = total.astype(BF16)

        tiles(t_rows, 16, tile)

        @pl.when(ring_of(i) != 0)
        def _():
            cz_copy(i).start()

    def finish(kind, out):
        far = range(1, planes) if kind == 0 else range(planes, count - 1)
        near = 0 if kind == 0 else count - 1
        for i in far:
            cz_copy(i).wait()

        def tile(at, size):
            here = pl.ds(at, size)
            total = gt[near, 0, here, :].astype(F32)
            for i in far:
                total = total + cz[i, here, :].astype(F32)
            out[here, :] = total.astype(BF16)

        tiles(t_rows, 16, tile)

    def live(i, body):
        @pl.when(jnp.logical_and(i >= 0, i < count))
        def _():
            body(i)

    def tick(i, carry):
        live(i, stage_z)
        live(i - 1, stage_y)
        live(i, lambda i: select(i, 0))
        live(i - 4, stage_out)
        live(i - 3, stage_act)
        live(i - 2, stage_in)
        live(i - 6, stage_cy)
        live(i - 5, stage_cx)
        return carry

    lax.fori_loop(0, count + 4, tick, 0)

    pairs = [((i + 1) % planes, i + planes) for i in range(planes)]

    def down_tile(at, size):
        total = None
        for a, b in pairs:
            term = mm(hid[a, :, pl.ds(at, size)], rows[b], 0, 0)
            total = term if total is None else total + term
        wd[pl.ds(at, size), :] = total.astype(BF16)

    tiles(ff, 128, down_tile)
    down_out = pltpu.make_async_copy(wd, grad_down.at[0], loc.at[3])
    down_out.start()

    stage_cy(count - 2)
    stage_cx(count - 1)

    def up_tile(at, size):
        total = None
        for a, b in pairs:
            term = mm(rows[a, :, pl.ds(at, size)], hid[b], 0, 0)
            total = term if total is None else total + term
        wu[pl.ds(at, size), :] = total.astype(BF16)

    tiles(feat, 256, up_tile)
    up_out = pltpu.make_async_copy(wu, grad_up.at[0], loc.at[2])
    up_out.start()

    stage_cy(count - 1)
    finish(0, mixed)
    finish(1, dtok)
    for i in range(1, planes):
        z_copy(i, tok).wait_send()
        mz_copy(i).wait_send()
    for i in range(planes, count - 1):
        z_copy(i, dmix).wait_send()
    down_out.wait()
    up_out.wait()


def per_device(tokens, gates, expert_ids, d_mixed, w_up, w_down):
    t_rows, feat = tokens.shape
    top = expert_ids.shape[1]
    ff = w_up.shape[2]
    groups = lax.axis_size("expert")
    nd = lax.axis_size("dp")
    hot_rows = t_rows // 2
    cold_rows = (t_rows * top - hot_rows + groups - 2) // (groups - 1)
    cap = max(hot_rows, cold_rows)
    planes = groups // 4
    count = 2 * planes
    half, chunk = 2 * cap, 4 * cap
    share = chunk // nd
    cfg = (groups, nd, t_rows, top, feat, ff, cap)
    dma = pltpu.SemaphoreType.DMA
    vm = pltpu.VMEM
    scratch = [
        vm((count, 2, t_rows, feat), BF16),
        vm((count, half, feat), BF16),
        vm((count, chunk, feat), BF16),
        vm((feat, ff), BF16),
        vm((ff, feat), BF16),
        vm((2, chunk, ff), BF16),
        vm((count, nd - 1, share, ff), BF16),
        vm((count, chunk, ff), BF16),
        vm((planes, share, ff), F32),
        vm((2, half, feat), BF16),
        vm((count, half, feat), BF16),
        vm((count, t_rows, feat), BF16),
        vm((count, t_rows, feat), BF16),
        vm((planes, 2, 2 * groups, t_rows), F32),
        vm((planes, 2, 2 * groups, t_rows), F32),
    ]
    for shape in (
        [(count,)] * 2 + [(planes,)] * 2 + [(count,)] * 2 + [(planes,)] * 2
        + [(count, 2)] * 2 + [(planes, 2)] * 2 + [(count, nd - 1)] * 4 + [(count,)] * 6 + [(4,)]
    ):
        scratch.append(dma(shape))
    pairs = groups * cap
    space = pl.BlockSpec(memory_space=pl.ANY)
    vmem = pl.BlockSpec(memory_space=pltpu.VMEM)
    return pl.pallas_call(
        functools.partial(kernel, cfg),
        out_shape=(
            jax.ShapeDtypeStruct((t_rows, feat), BF16),
            jax.ShapeDtypeStruct((t_rows, feat), BF16),
            jax.ShapeDtypeStruct(w_up.shape, BF16),
            jax.ShapeDtypeStruct(w_down.shape, BF16),
        ),
        in_specs=[space, vmem, vmem, space, space, space],
        out_specs=(vmem, vmem, space, space),
        scratch_shapes=scratch,
        compiler_params=pltpu.CompilerParams(
            collective_id=0, has_side_effects=True, vmem_limit_bytes=60 * 2**20
        ),
        cost_estimate=pl.CostEstimate(
            flops=12 * pairs * feat * ff, bytes_accessed=8 * feat * ff, transcendentals=pairs * ff
        ),
        name="moe_layer",
    )(tokens, gates, expert_ids, d_mixed, w_up, w_down)


def solution(mesh):
    in_specs = (
        P("expert", "dp"),
        P("expert", None),
        P("expert", None),
        P("expert", "dp"),
        P("expert", "dp", None),
        P("expert", None, "dp"),
    )
    out_specs = (
        P("expert", "dp"),
        P("expert", "dp"),
        P("expert", "dp", None),
        P("expert", None, "dp"),
    )
    return jax.shard_map(
        per_device, mesh=mesh, in_specs=in_specs, out_specs=out_specs, check_vma=False
    )
```

time: 504 us -> 271 us (0.54)
  waiting for transfers between devices: 335 us -> 0 us
  Pallas kernels: 0 us -> 257 us
  matrix products: 54 us -> 0 us
  local copies, waits for them, and re-layouts: 49.6 us -> 13.4 us
  starting transfers between devices: 26.3 us -> 0 us
  other arithmetic: 24.6 us -> 0 us
  between operations: 13.9 us -> 0.64 us
    all_to_all x4 -> x0, waiting for transfers between devices: 299 us -> none  [the longest x1 88.2 us: per_device(): lax.all_to_all(scaled_in.reshape(groups, capacity, features), 'expert', s...]
    pallas_call x0 -> x1, Pallas kernels: none -> 257 us  [per_device(): pl.pallas_call(functools.partial(kernel, cfg), out_shape=(jax.ShapeDtypeS...]
    dot_general x6 -> x0, matrix products: 54 us -> none  [the longest x2 18.6 us: transposed_product(): lax.dot_general(row_block, first_weight, contract, preferred_element_type...]
    gather x4 -> x0, local copies, waits for them, and re-layouts: 40.6 us -> none  [the longest x1 11.6 us: per_device(): scaled_in = jnp.concatenate([scaled, zero_row], 0)[source]]
    all_to_all x4 -> x0, starting transfers between devices: 26 us -> none  [the longest x1 7.3 us: per_device(): lax.all_to_all(scaled_in.reshape(groups, capacity, features), 'expert', s...]
    all_gather x2 -> x0, waiting for transfers between devices: 25.7 us -> none  [the longest x1 13.8 us: per_device(): lax.all_gather(grad_share, 'dp', axis=0, tiled=True)]
    reduce_sum x3 -> x0, other arithmetic: 13.2 us -> none  [the longest x1 7.32 us: per_device(): mixed_out = jnp.sum(gates[:, :, None] * pair_out, 1).astype(jnp.bfloat16)]
    unnamed x8, local copies, waits for them, and re-layouts: 1.58 us -> 13.4 us
  transfers between devices with their start and end apart: 8 -> 0, of which waited for: 7 -> 0; matrix products, arithmetic and copies ran while one was open for 14% -> 0% of each run, Pallas kernels for 0% -> 0%
where the time goes in v1:
time: 271 us
  Pallas kernels  257 us (95%)
  local copies, waits for them, and re-layouts  13.4 us (5%)
    pallas_call x1, Pallas kernels, per_device(): pl.pallas_call(functools.partial(kernel, cfg), out_shape=(jax.ShapeDtypeS...  257 us
    unnamed x8, local copies, waits for them, and re-layouts  13.4 us

profile of v1, /device:TPU:12, one launch (start us, length us, event | category | flops | bytes accessed | tf_op | source)
XLA Modules:
  0.0 270.8 jit_solution(3792047526851394512)
XLA Ops:
  0.6 1.4 copy.10.gates
  2.0 1.4 copy.11.ids
  3.5 256.7 %moe_layer.1 = (bf16[128,2048]{1,0:T(8,128)(2,1)}, bf16[128,2048]{1,0:T(8,128)(2,1)}, bf16[1,2048,1024]{2,1,0:T(8,128)(2,1)}, bf16[1,1024,2048]{2,1,0:T(8,128)(2,1)}) custom-call(bf16[128,2048]{1,0:T(8,128)(2,1)} %tok.1, f32[128,8]{1,0:T(8,128)} %copy.10.gates, s32[128,8]{1,0:T(8,128)} %copy.11.ids, bf16[128,2048]{1,0:T(8,128)(2,1)} %dmix.1, ...), custom_call_target="tpu_custom_call" | custom-call | flops 25769803776 | bytes 16777216 | tf_op jit(solution)/shard_map/moe_layer/pallas_call | solution.py:449
  260.2 1.9 copy.16
  262.1 1.9 copy.17
  263.9 0.0 copy-start
  264.0 4.8 %copy.18 = bf16[1,2048,1024]{2,1,0:T(8,128)(2,1)} copy(bf16[1,2048,1024]{2,1,0:T(8,128)(2,1)} %get-tuple-element.10) | data formatting | bytes 8388608
  268.8 0.0 copy-done
  268.8 2.0 copy.19
Async XLA Ops:
  263.9 4.8 %copy-start = (bf16[1,1024,2048]{2,1,0:T(8,128)(2,1)S(1)}, bf16[1,1024,2048]{2,1,0:T(8,128)(2,1)}, u32[]{:S(2)}) copy-start(bf16[1,1024,2048]{2,1,0:T(8,128)(2,1)} %get-tuple-element.11) | copy-start | bytes 12582916

commit v2 on v1

--- a/solution.py
+++ b/solution.py
@@ -28,6 +28,15 @@
     while bit < limit:
         on = (mask // bit) % 2
         result = result + bit * on * (1 - 2 * ((value // bit) % 2))
+        bit *= 2
+    return result
+
+
+def differ(a, b, limit):
+    result = 0
+    bit = 1
+    while bit < limit:
+        result = result + bit * ((a // bit + b // bit) % 2)
         bit *= 2
     return result
 
@@ -57,7 +66,14 @@
     e_y = e + 2 - 4 * y
 
     def ring_of(i):
-        return (i + i // planes) % planes
+        r = (i + i // planes) % planes
+        if planes == 4:
+            inner = (z % 3 + 2) // 3
+            r = r + inner * (r // 2) * (5 - 2 * r)
+        return r
+
+    def slot_of(i):
+        return (i // planes) * planes + ring_of(i)
 
     def z_peer(r):
         return flip(z, r, planes) * 4 + y * 2 + x
@@ -69,11 +85,38 @@
             device_id=where, device_id_type=MESH,
         )
 
-    def z_copy(i, src):
-        return send(src, gt.at[i, 0], zs.at[i], zr.at[i], z_peer(ring_of(i)))
-
-    def mz_copy(i):
-        return send(mt.at[0, 0], mt.at[i, 0], mzs.at[i], mzr.at[i], z_peer(ring_of(i)))
+    def z_next(s, origin, way):
+        there = z + 1 - 2 * way
+        return there * 4 + y * 2 + x, (s // planes) * planes + differ(origin, there, planes)
+
+    def z_copy(s, origin, way, src=None):
+        peer, slot = z_next(s, origin, way)
+        src = gt.at[s, 0] if src is None else src
+        return send(src, gt.at[slot, 0], zs.at[s, way], zr.at[slot], peer)
+
+    def mz_copy(s, origin, way):
+        peer, slot = z_next(s, origin, way)
+        return send(mt.at[s, 0], mt.at[slot, 0], mzs.at[s, way], mzr.at[slot], peer)
+
+    def onward(s, act):
+        origin = flip(z, s % planes, planes)
+
+        @pl.when(jnp.logical_and(origin < z, z < planes - 1))
+        def _():
+            act(origin, 0)
+
+        @pl.when(jnp.logical_and(origin > z, z > 0))
+        def _():
+            act(origin, 1)
+
+    def outward(act):
+        @pl.when(z < planes - 1)
+        def _():
+            act(z, 0)
+
+        @pl.when(z > 0)
+        def _():
+            act(z, 1)
 
     def y_copy(i):
         return send(gt.at[i, 0], gt.at[i, 1], ys.at[i], yr.at[i], e_y)
@@ -90,10 +133,10 @@
     def mx_copy(i, yy):
         return send(mt.at[i, yy], mx.at[i, yy], mxs.at[i, yy], mxr.at[i, yy], e_x)
 
-    def rs_copy(i, o):
+    def rs_copy(i, h, o):
         peer = (me + o) % nd
         return send(
-            part.at[i % 2, pl.ds(pl.multiple_of(peer * share, share), share)],
+            part.at[h, pl.ds(pl.multiple_of(peer * share, share), share)],
             rsbuf.at[i, o - 1], rss.at[i, o - 1], rsr.at[i, o - 1], dp=peer,
         )
 
@@ -101,17 +144,18 @@
         mine = hid.at[i, pl.ds(pl.multiple_of(me * share, share), share)]
         return send(mine, mine, ags.at[i, o - 1], agr.at[i, o - 1], dp=(me + o) % nd)
 
-    def cx_copy(i):
-        return send(sx.at[i], cx.at[i], cxs.at[i], cxr.at[i], e_x)
+    def cx_copy(i, yy):
+        here = pl.ds(yy * cap, cap)
+        return send(sx.at[i, here], cx.at[i, here], cxs.at[i, yy], cxr.at[i, yy], e_x)
 
     def cy_copy(i):
         return send(gt.at[i, 1], cy.at[i], cys.at[i], cyr.at[i], e_y)
 
     def cz_copy(i):
-        return send(gt.at[i, 0], cz.at[i], czs.at[i], czr.at[i], z_peer(ring_of(i)))
+        return send(gt.at[i, 0], cz.at[i], czs.at[i], czr.at[i], z_peer(i % planes))
 
     tok_in = pltpu.make_async_copy(tok, gt.at[0, 0], loc.at[0])
-    dmix_in = pltpu.make_async_copy(dmix, gt.at[count - 1, 0], loc.at[1])
+    dmix_in = pltpu.make_async_copy(dmix, gt.at[planes, 0], loc.at[1])
     wu_in = pltpu.make_async_copy(w_up.at[0], wu, loc.at[2])
     wd_in = pltpu.make_async_copy(w_down.at[0], wd, loc.at[3])
     tok_in.start()
@@ -127,24 +171,22 @@
         pl.semaphore_signal(barrier, inc=1, device_id=peer, device_id_type=MESH)
     pl.semaphore_wait(barrier, len(peers))
 
-    for i in range(1, planes):
-        z_copy(i, tok).start()
-
+    outward(lambda origin, way: z_copy(0, origin, way, tok).start())
+
+    expert_row = lax.broadcasted_iota(jnp.int32, (groups, t_rows), 0)
+    chosen = jnp.zeros((groups, t_rows), F32)
+    weight = jnp.zeros((groups, t_rows), F32)
+    for k in range(top):
+        hit = ids[k : k + 1, :] == expert_row
+        chosen = chosen + jnp.where(hit, 1.0, 0.0)
+        weight = weight + jnp.where(hit, gates[k : k + 1, :], 0.0)
     lane = lax.broadcasted_iota(jnp.int32, (t_rows, t_rows), 1)
     row = lax.broadcasted_iota(jnp.int32, (t_rows, t_rows), 0)
-    chosen = jnp.zeros((t_rows, t_rows), F32)
-    weight = jnp.zeros((t_rows, t_rows), F32)
-    for k in range(top):
-        hit = ids[:, k : k + 1] == lane
-        chosen = chosen + jnp.where(hit, 1.0, 0.0)
-        weight = weight + jnp.where(hit, gates[:, k : k + 1], 0.0)
-    before = jnp.where(lane < row, 1.0, 0.0).astype(BF16)
-    place = mm(before, chosen.astype(BF16), 1, 0)
-    place = jnp.where(chosen > 0.0, place, -1.0)
-    mt[0, 0, :groups, :] = jnp.transpose(place)[:groups]
-    mt[0, 0, groups:, :] = jnp.transpose(weight)[:groups]
-    for i in range(1, planes):
-        mz_copy(i).start()
+    before = jnp.where(row < lane, 1.0, 0.0).astype(BF16)
+    place = mm(chosen.astype(BF16), before, 1, 0)
+    mt[0, 0, :groups, :] = jnp.where(chosen > 0.0, place, -1.0)
+    mt[0, 0, groups:, :] = weight
+    outward(lambda origin, way: mz_copy(0, origin, way).start())
 
     slot = lax.broadcasted_iota(jnp.int32, (cap, t_rows), 0).astype(F32)
 
@@ -154,7 +196,7 @@
         return jnp.where(hot, 1.0, 0.0).astype(BF16), gate
 
     def select(i, yy):
-        r = ring_of(i)
+        r = i % planes
         hot_n, gate_n = pick(mt.at[r, yy], e_x)
         hot_o, gate_o = pick(mt.at[r, yy], e)
         hot = jnp.concatenate([hot_n, hot_o], 0)
@@ -179,17 +221,19 @@
         def _():
             tok_in.wait()
 
-        @pl.when(i == count - 1)
+        @pl.when(i == planes)
         def _():
             dmix_in.wait()
 
-        @pl.when(ring_of(i) != 0)
-        def _():
-            z_copy(i, tok).wait_recv()
+        @pl.when(i % planes != 0)
+        def _():
+            send(gt.at[i, 0], gt.at[i, 0], zs.at[i, 0], zr.at[i], e_x).wait_recv()
+            onward(i, lambda origin, way: z_copy(i, origin, way).start())
 
             @pl.when(i < planes)
             def _():
-                mz_copy(i).wait_recv()
+                send(mt.at[i, 0], mt.at[i, 0], mzs.at[i, 0], mzr.at[i], e_x).wait_recv()
+                onward(i, lambda origin, way: mz_copy(i, origin, way).start())
 
         y_copy(i).start()
 
@@ -197,9 +241,9 @@
         def _():
             my_copy(i).start()
 
-        @pl.when(i < planes - 1)
-        def _():
-            z_copy(i + planes, dmix).start()
+        @pl.when(i == 1)
+        def _():
+            outward(lambda origin, way: z_copy(planes, origin, way, dmix).start())
 
     def stage_y(i):
         y_copy(i).wait()
@@ -210,7 +254,7 @@
 
         select(i, 1)
 
-    def stage_in(i):
+    def stage_in(i, h):
         for yy in range(2):
             x_copy(i, yy).wait()
 
@@ -224,7 +268,7 @@
                 wu_in.wait()
 
             def tile(at, size):
-                part[i % 2, :, pl.ds(at, size)] = mm(
+                part[h, :, pl.ds(at, size)] = mm(
                     rows[i], wu[:, pl.ds(at, size)], 1, 0
                 ).astype(BF16)
 
@@ -233,24 +277,24 @@
         @pl.when(i >= planes)
         def _():
             def tile(at, size):
-                part[i % 2, :, pl.ds(at, size)] = mm(
+                part[h, :, pl.ds(at, size)] = mm(
                     rows[i], wd[pl.ds(at, size), :], 1, 1
                 ).astype(BF16)
 
             tiles(ff, 256, tile)
 
         for o in range(1, nd):
-            rs_copy(i, o).start()
-
-    def stage_act(i):
+            rs_copy(i, h, o).start()
+
+    def stage_act(i, h):
         for o in range(1, nd):
-            rs_copy(i, o).wait()
-        r = ring_of(i)
+            rs_copy(i, h, o).wait()
+        r = i % planes
         base = me * share
 
         def tile(at, size):
             here = pl.ds(pl.multiple_of(base + at, size), size)
-            total = part[i % 2, here, :].astype(F32)
+            total = part[h, here, :].astype(F32)
             for o in range(1, nd):
                 total = total + rsbuf[i, o - 1, pl.ds(at, size), :].astype(F32)
 
@@ -269,13 +313,13 @@
         for o in range(1, nd):
             ag_copy(i, o).start()
 
-    def stage_out(i):
+    def stage_out(i, h):
         for o in range(1, nd):
             ag_copy(i, o).wait()
 
         def store(at, size, got):
             got = got.astype(BF16)
-            own[i % 2, :, pl.ds(at, size)] = got[:half]
+            own[h, :, pl.ds(at, size)] = got[:half]
             sx[i, :, pl.ds(at, size)] = got[half:]
 
         @pl.when(i < planes)
@@ -300,42 +344,55 @@
 
             tiles(feat, 256, tile)
 
-        cx_copy(i).start()
-
-    def stage_cx(i):
-        cx_copy(i).wait()
-        r = ring_of(i)
-        for yy in (1, 0):
-            hot = jnp.concatenate([pick(mt.at[r, yy], e)[0], pick(mt.at[r, yy], e_x)[0]], 0)
-
-            def tile(at, size):
-                there = slice(yy * cap, (yy + 1) * cap)
-                data = jnp.concatenate(
-                    [own[i % 2, there, pl.ds(at, size)], cx[i, there, pl.ds(at, size)]], 0
-                )
-                gt[i, yy, :, pl.ds(at, size)] = mm(hot, data, 0, 0).astype(BF16)
-
-            tiles(feat, 512, tile)
-            if yy == 1:
-                cy_copy(i).start()
-
-    def stage_cy(i):
+        cx_copy(i, 1).start()
+        cx_copy(i, 0).start()
+
+    def placed(i, h, yy):
+        r = i % planes
+        hot = jnp.concatenate([pick(mt.at[r, yy], e)[0], pick(mt.at[r, yy], e_x)[0]], 0)
+        there = slice(yy * cap, (yy + 1) * cap)
+
+        def tile(at, size):
+            data = jnp.concatenate(
+                [own[h, there, pl.ds(at, size)], cx[i, there, pl.ds(at, size)]], 0
+            )
+            return mm(hot, data, 0, 0)
+
+        return tile
+
+    def stage_cx(i, h):
+        cx_copy(i, 1).wait()
+        sums = placed(i, h, 1)
+
+        def tile(at, size):
+            gt[i, 1, :, pl.ds(at, size)] = sums(at, size).astype(BF16)
+
+        tiles(feat, 512, tile)
+        cy_copy(i).start()
+
+    def stage_cy(i, h):
+        cx_copy(i, 0).wait()
         cy_copy(i).wait()
+
+        @pl.when(i % planes != 0)
+        def _():
+            onward(i, lambda origin, way: z_copy(i, origin, way).wait_send())
+
+        sums = placed(i, h, 0)
 
         def tile(at, size):
             here = pl.ds(at, size)
-            total = gt[i, 0, here, :].astype(F32) + cy[i, here, :].astype(F32)
-            gt[i, 0, here, :] = total.astype(BF16)
-
-        tiles(t_rows, 16, tile)
-
-        @pl.when(ring_of(i) != 0)
+            gt[i, 0, :, here] = (sums(at, size) + cy[i, :, here].astype(F32)).astype(BF16)
+
+        tiles(feat, 512, tile)
+
+        @pl.when(i % planes != 0)
         def _():
             cz_copy(i).start()
 
     def finish(kind, out):
-        far = range(1, planes) if kind == 0 else range(planes, count - 1)
-        near = 0 if kind == 0 else count - 1
+        near = kind * planes
+        far = range(near + 1, near + planes)
         for i in far:
             cz_copy(i).wait()
 
@@ -351,22 +408,22 @@
     def live(i, body):
         @pl.when(jnp.logical_and(i >= 0, i < count))
         def _():
-            body(i)
+            body(slot_of(i), i % 2)
 
     def tick(i, carry):
-        live(i, stage_z)
-        live(i - 1, stage_y)
-        live(i, lambda i: select(i, 0))
-        live(i - 4, stage_out)
-        live(i - 3, stage_act)
-        live(i - 2, stage_in)
         live(i - 6, stage_cy)
         live(i - 5, stage_cx)
+        live(i - 4, stage_act)
+        live(i - 4, stage_out)
+        live(i - 2, lambda s, h: stage_y(s))
+        live(i - 3, stage_in)
+        live(i, lambda s, h: stage_z(s))
+        live(i, lambda s, h: select(s, 0))
         return carry
 
     lax.fori_loop(0, count + 4, tick, 0)
 
-    pairs = [((i + 1) % planes, i + planes) for i in range(planes)]
+    pairs = [(i, i + planes) for i in range(planes)]
 
     def down_tile(at, size):
         total = None
@@ -379,8 +436,8 @@
     down_out = pltpu.make_async_copy(wd, grad_down.at[0], loc.at[3])
     down_out.start()
 
-    stage_cy(count - 2)
-    stage_cx(count - 1)
+    stage_cy(slot_of(count - 2), count % 2)
+    stage_cx(slot_of(count - 1), (count - 1) % 2)
 
     def up_tile(at, size):
         total = None
@@ -393,14 +450,14 @@
     up_out = pltpu.make_async_copy(wu, grad_up.at[0], loc.at[2])
     up_out.start()
 
-    stage_cy(count - 1)
+    stage_cy(slot_of(count - 1), (count - 1) % 2)
     finish(0, mixed)
     finish(1, dtok)
+    outward(lambda origin, way: z_copy(0, origin, way, tok).wait_send())
+    outward(lambda origin, way: z_copy(planes, origin, way, dmix).wait_send())
+    outward(lambda origin, way: mz_copy(0, origin, way).wait_send())
     for i in range(1, planes):
-        z_copy(i, tok).wait_send()
-        mz_copy(i).wait_send()
-    for i in range(planes, count - 1):
-        z_copy(i, dmix).wait_send()
+        onward(i, lambda origin, way, i=i: mz_copy(i, origin, way).wait_send())
     down_out.wait()
     up_out.wait()
 
@@ -439,8 +496,8 @@
         vm((planes, 2, 2 * groups, t_rows), F32),
     ]
     for shape in (
-        [(count,)] * 2 + [(planes,)] * 2 + [(count,)] * 2 + [(planes,)] * 2
-        + [(count, 2)] * 2 + [(planes, 2)] * 2 + [(count, nd - 1)] * 4 + [(count,)] * 6 + [(4,)]
+        [(count, 2), (count,), (planes, 2), (planes,)] + [(count,)] * 2 + [(planes,)] * 2
+        + [(count, 2)] * 2 + [(planes, 2)] * 2 + [(count, nd - 1)] * 4 + [(count, 2)] * 2 + [(count,)] * 4 + [(4,)]
     ):
         scratch.append(dma(shape))
     pairs = groups * cap
@@ -464,7 +521,7 @@
             flops=12 * pairs * feat * ff, bytes_accessed=8 * feat * ff, transcendentals=pairs * ff
         ),
         name="moe_layer",
-    )(tokens, gates, expert_ids, d_mixed, w_up, w_down)
+    )(tokens, gates.T, expert_ids.T, d_mixed, w_up, w_down)
 
 
 def solution(mesh):

time: 271 us -> 240 us (0.89); the launches traced: 271 us -> 236 us
  Pallas kernels: 257 us -> 225 us
  local copies, waits for them, and re-layouts: 13.4 us -> 10.6 us
    pallas_call x1, Pallas kernels: 257 us -> 225 us  [per_device(): pl.pallas_call(functools.partial(kernel, cfg), out_shape=(jax.ShapeDtypeS...]
    unnamed x8 -> x6, local copies, waits for them, and re-layouts: 13.4 us -> 10.6 us
where the time goes in v2:
time: 240 us; the launch traced here: 236 us
  Pallas kernels  225 us (94%)
  local copies, waits for them, and re-layouts  10.6 us (4%)
    pallas_call x1, Pallas kernels, per_device(): pl.pallas_call(functools.partial(kernel, cfg), out_shape=(jax.ShapeDtypeS...  225 us
    unnamed x6, local copies, waits for them, and re-layouts  10.6 us

profile of v2, /device:TPU:12, one launch (start us, length us, event | category | flops | bytes accessed | tf_op | source)
XLA Modules:
  0.0 236.2 jit_solution(1815813133883886021)
XLA Ops:
  0.6 225.0 %moe_layer.1 = (bf16[128,2048]{1,0:T(8,128)(2,1)}, bf16[128,2048]{1,0:T(8,128)(2,1)}, bf16[1,2048,1024]{2,1,0:T(8,128)(2,1)}, bf16[1,1024,2048]{2,1,0:T(8,128)(2,1)}) custom-call(bf16[128,2048]{1,0:T(8,128)(2,1)} %tok.1, f32[8,128]{1,0:T(8,128)} %bitcast.2, s32[8,128]{1,0:T(8,128)} %bitcast.3, bf16[128,2048]{1,0:T(8,128)(2,1)} %dmix.1, ...), custom_call_target="tpu_custom_call" | custom-call | flops 25769803776 | bytes 16777216 | tf_op jit(solution)/shard_map/moe_layer/pallas_call | solution.py:506
  225.6 1.9 copy.14
  227.5 1.9 copy.15
  229.4 0.0 copy-start
  229.4 4.8 %copy.16 = bf16[1,2048,1024]{2,1,0:T(8,128)(2,1)} copy(bf16[1,2048,1024]{2,1,0:T(8,128)(2,1)} %get-tuple-element.10) | data formatting | bytes 8388608
  234.2 0.0 copy-done
  234.2 2.0 copy.17
Async XLA Ops:
  229.4 4.8 %copy-start = (bf16[1,1024,2048]{2,1,0:T(8,128)(2,1)S(1)}, bf16[1,1024,2048]{2,1,0:T(8,128)(2,1)}, u32[]{:S(2)}) copy-start(bf16[1,1024,2048]{2,1,0:T(8,128)(2,1)} %get-tuple-element.11) | copy-start | bytes 12582916

commit v3 on v2

--- a/solution.py
+++ b/solution.py
@@ -66,8 +66,10 @@
     e_y = e + 2 - 4 * y
 
     def ring_of(i):
-        r = (i + i // planes) % planes
+        kind, m = i // planes, i % planes
+        r = (m + kind) % planes
         if planes == 4:
+            r = m + kind * (2 - 2 * m + (m // 2) * (3 - 2 * (m % 2)))
             inner = (z % 3 + 2) // 3
             r = r + inner * (r // 2) * (5 - 2 * r)
         return r
@@ -216,7 +218,7 @@
         def _():
             mx_copy(i, yy).start()
 
-    def stage_z(i):
+    def stage_z(i, order):
         @pl.when(i == 0)
         def _():
             tok_in.wait()
@@ -241,7 +243,7 @@
         def _():
             my_copy(i).start()
 
-        @pl.when(i == 1)
+        @pl.when(order == planes - 1)
         def _():
             outward(lambda origin, way: z_copy(planes, origin, way, dmix).start())
 
@@ -411,14 +413,14 @@
             body(slot_of(i), i % 2)
 
     def tick(i, carry):
+        live(i - 4, stage_act)
         live(i - 6, stage_cy)
         live(i - 5, stage_cx)
-        live(i - 4, stage_act)
         live(i - 4, stage_out)
+        live(i, lambda s, h: stage_z(s, i))
+        live(i, lambda s, h: select(s, 0))
         live(i - 2, lambda s, h: stage_y(s))
         live(i - 3, stage_in)
-        live(i, lambda s, h: stage_z(s))
-        live(i, lambda s, h: select(s, 0))
         return carry
 
     lax.fori_loop(0, count + 4, tick, 0)
@@ -432,7 +434,7 @@
             total = term if total is None else total + term
         wd[pl.ds(at, size), :] = total.astype(BF16)
 
-    tiles(ff, 128, down_tile)
+    tiles(ff, 256, down_tile)
     down_out = pltpu.make_async_copy(wd, grad_down.at[0], loc.at[3])
     down_out.start()
 
@@ -446,12 +448,12 @@
             total = term if total is None else total + term
         wu[pl.ds(at, size), :] = total.astype(BF16)
 
-    tiles(feat, 256, up_tile)
+    tiles(feat, 512, up_tile)
     up_out = pltpu.make_async_copy(wu, grad_up.at[0], loc.at[2])
     up_out.start()
 
+    finish(0, mixed)
     stage_cy(slot_of(count - 1), (count - 1) % 2)
-    finish(0, mixed)
     finish(1, dtok)
     outward(lambda origin, way: z_copy(0, origin, way, tok).wait_send())
     outward(lambda origin, way: z_copy(planes, origin, way, dmix).wait_send())

time: 240 us -> 234 us (0.975)
  Pallas kernels: 225 us -> 218 us
    pallas_call x1, Pallas kernels: 225 us -> 218 us  [per_device(): pl.pallas_call(functools.partial(kernel, cfg), out_shape=(jax.ShapeDtypeS...]
where the time goes in v3:
time: 234 us; the launch traced here: 229 us
  Pallas kernels  218 us (93%)
  local copies, waits for them, and re-layouts  10.6 us (5%)
    pallas_call x1, Pallas kernels, per_device(): pl.pallas_call(functools.partial(kernel, cfg), out_shape=(jax.ShapeDtypeS...  218 us
    unnamed x6, local copies, waits for them, and re-layouts  10.6 us

profile of v3, /device:TPU:12, one launch (start us, length us, event | category | flops | bytes accessed | tf_op | source)
XLA Modules:
  0.0 229.4 jit_solution(6847692879910515957)
XLA Ops:
  0.6 218.1 %moe_layer.1 = (bf16[128,2048]{1,0:T(8,128)(2,1)}, bf16[128,2048]{1,0:T(8,128)(2,1)}, bf16[1,2048,1024]{2,1,0:T(8,128)(2,1)}, bf16[1,1024,2048]{2,1,0:T(8,128)(2,1)}) custom-call(bf16[128,2048]{1,0:T(8,128)(2,1)} %tok.1, f32[8,128]{1,0:T(8,128)} %bitcast.2, s32[8,128]{1,0:T(8,128)} %bitcast.3, bf16[128,2048]{1,0:T(8,128)(2,1)} %dmix.1, ...), custom_call_target="tpu_custom_call" | custom-call | flops 25769803776 | bytes 16777216 | tf_op jit(solution)/shard_map/moe_layer/pallas_call | solution.py:508
  218.8 1.9 copy.14
  220.6 1.9 copy.15
  222.5 0.0 copy-start
  222.5 4.8 %copy.16 = bf16[1,2048,1024]{2,1,0:T(8,128)(2,1)} copy(bf16[1,2048,1024]{2,1,0:T(8,128)(2,1)} %get-tuple-element.10) | data formatting | bytes 8388608
  227.3 0.0 copy-done
  227.3 2.0 copy.17
Async XLA Ops:
  222.5 4.8 %copy-start = (bf16[1,1024,2048]{2,1,0:T(8,128)(2,1)S(1)}, bf16[1,1024,2048]{2,1,0:T(8,128)(2,1)}, u32[]{:S(2)}) copy-start(bf16[1,1024,2048]{2,1,0:T(8,128)(2,1)} %get-tuple-element.11) | copy-start | bytes 12582916

commit v4 on v3

--- a/solution.py
+++ b/solution.py
@@ -48,7 +48,7 @@
 def kernel(
     cfg,
     tok, gates, ids, dmix, w_up, w_down,
-    mixed, dtok, grad_up, grad_down,
+    both, grad_up, grad_down,
     gt, sx, rows, wu, wd, part, rsbuf, hid, pre, own, cx, cy, cz, mt, mx,
     zs, zr, mzs, mzr, ys, yr, mys, myr, xs, xr, mxs, mxr,
     rss, rsr, ags, agr, cxs, cxr, cys, cyr, czs, czr, loc,
@@ -175,6 +175,9 @@
 
     outward(lambda origin, way: z_copy(0, origin, way, tok).start())
 
+    tok_in.wait()
+    y_copy(0).start()
+
     expert_row = lax.broadcasted_iota(jnp.int32, (groups, t_rows), 0)
     chosen = jnp.zeros((groups, t_rows), F32)
     weight = jnp.zeros((groups, t_rows), F32)
@@ -219,10 +222,6 @@
             mx_copy(i, yy).start()
 
     def stage_z(i, order):
-        @pl.when(i == 0)
-        def _():
-            tok_in.wait()
-
         @pl.when(i == planes)
         def _():
             dmix_in.wait()
@@ -237,7 +236,9 @@
                 send(mt.at[i, 0], mt.at[i, 0], mzs.at[i, 0], mzr.at[i], e_x).wait_recv()
                 onward(i, lambda origin, way: mz_copy(i, origin, way).start())
 
-        y_copy(i).start()
+        @pl.when(i != 0)
+        def _():
+            y_copy(i).start()
 
         @pl.when(i < planes)
         def _():
@@ -392,18 +393,16 @@
         def _():
             cz_copy(i).start()
 
-    def finish(kind, out):
-        near = kind * planes
-        far = range(near + 1, near + planes)
-        for i in far:
+    def finish_tokens():
+        for i in range(1, planes):
             cz_copy(i).wait()
 
         def tile(at, size):
             here = pl.ds(at, size)
-            total = gt[near, 0, here, :].astype(F32)
-            for i in far:
+            total = gt[0, 0, here, :].astype(F32)
+            for i in range(1, planes):
                 total = total + cz[i, here, :].astype(F32)
-            out[here, :] = total.astype(BF16)
+            both[0, here, :] = total.astype(BF16)
 
         tiles(t_rows, 16, tile)
 
@@ -452,9 +451,22 @@
     up_out = pltpu.make_async_copy(wu, grad_up.at[0], loc.at[2])
     up_out.start()
 
-    finish(0, mixed)
-    stage_cy(slot_of(count - 1), (count - 1) % 2)
-    finish(1, dtok)
+    finish_tokens()
+
+    cx_copy(planes, 0).wait()
+    cy_copy(planes).wait()
+    for s in range(planes + 1, count):
+        cz_copy(s).wait()
+    sums = placed(planes, (count - 1) % 2, 0)
+
+    def last_tile(at, size):
+        here = pl.ds(at, size)
+        total = sums(at, size) + cy[planes, :, here].astype(F32)
+        for s in range(planes + 1, count):
+            total = total + cz[s, :, here].astype(F32)
+        both[1, :, here] = total.astype(BF16)
+
+    tiles(feat, 512, last_tile)
     outward(lambda origin, way: z_copy(0, origin, way, tok).wait_send())
     outward(lambda origin, way: z_copy(planes, origin, way, dmix).wait_send())
     outward(lambda origin, way: mz_copy(0, origin, way).wait_send())
@@ -505,16 +517,15 @@
     pairs = groups * cap
     space = pl.BlockSpec(memory_space=pl.ANY)
     vmem = pl.BlockSpec(memory_space=pltpu.VMEM)
-    return pl.pallas_call(
+    both, grad_up, grad_down = pl.pallas_call(
         functools.partial(kernel, cfg),
         out_shape=(
-            jax.ShapeDtypeStruct((t_rows, feat), BF16),
-            jax.ShapeDtypeStruct((t_rows, feat), BF16),
+            jax.ShapeDtypeStruct((2, t_rows, feat), BF16),
             jax.ShapeDtypeStruct(w_up.shape, BF16),
             jax.ShapeDtypeStruct(w_down.shape, BF16),
         ),
         in_specs=[space, vmem, vmem, space, space, space],
-        out_specs=(vmem, vmem, space, space),
+        out_specs=(vmem, space, space),
         scratch_shapes=scratch,
         compiler_params=pltpu.CompilerParams(
             collective_id=0, has_side_effects=True, vmem_limit_bytes=60 * 2**20
@@ -524,6 +535,7 @@
         ),
         name="moe_layer",
     )(tokens, gates.T, expert_ids.T, d_mixed, w_up, w_down)
+    return both[0], both[1], grad_up, grad_down
 
 
 def solution(mesh):

time: 234 us -> 233 us (level)
    unnamed x6 -> x4, local copies, waits for them, and re-layouts: 10.6 us -> 6.83 us
where the time goes in v4:
time: 233 us; the launch traced here: 228 us
  Pallas kernels  219 us (94%)
  local copies, waits for them, and re-layouts  9.11 us (4%)
    pallas_call x1, Pallas kernels, per_device(): pl.pallas_call(functools.partial(kernel, cfg), out_shape=(jax.ShapeDtypeS...  219 us
    unnamed x4, local copies, waits for them, and re-layouts  6.83 us

profile of v4, /device:TPU:12, one launch (start us, length us, event | category | flops | bytes accessed | tf_op | source)
XLA Modules:
  0.0 228.5 jit_solution(16757975575581161515)
XLA Ops:
  0.6 218.7 %moe_layer.1 = (bf16[2,128,2048]{2,1,0:T(8,128)(2,1)}, bf16[1,2048,1024]{2,1,0:T(8,128)(2,1)}, bf16[1,1024,2048]{2,1,0:T(8,128)(2,1)}) custom-call(bf16[128,2048]{1,0:T(8,128)(2,1)} %tok.1, f32[8,128]{1,0:T(8,128)} %bitcast.6, s32[8,128]{1,0:T(8,128)} %bitcast.7, bf16[128,2048]{1,0:T(8,128)(2,1)} %dmix.1, bf16[1,2048,1024]{2,1,0:T(8,128)(2,1)} %w_up.1, ...), custom_call_target="tpu_custom_call" | custom-call | flops 25769803776 | bytes 16777216 | tf_op jit(solution)/shard_map/moe_layer/pallas_call | solution.py:520
  219.4 2.3 slice_bitcast_fusion
  221.6 0.0 copy-start
  221.6 4.8 %copy.12 = bf16[1,2048,1024]{2,1,0:T(8,128)(2,1)} copy(bf16[1,2048,1024]{2,1,0:T(8,128)(2,1)} %get-tuple-element.18) | data formatting | bytes 8388608
  226.5 0.0 copy-done
  226.5 2.0 copy.13
Async XLA Ops:
  221.6 4.8 %copy-start = (bf16[1,1024,2048]{2,1,0:T(8,128)(2,1)S(1)}, bf16[1,1024,2048]{2,1,0:T(8,128)(2,1)}, u32[]{:S(2)}) copy-start(bf16[1,1024,2048]{2,1,0:T(8,128)(2,1)} %get-tuple-element.19) | copy-start | bytes 12582916
